TPU v7x, 512 devices: a whole 4x4x16 slice. The times are simulated.
512 devices in a mesh: amp: 64 (over y, z), int: 8 (over x, core).
Axes of the slice: x: 4, y: 4, z: 16, core: 2. Of those that a mesh axis runs over, the one named last changes fastest.
Arguments:
- amps: bfloat16 [512, 1024, 128], P('amp', 'int'), may hold values from -6 to 6
- integrals: bfloat16 [512, 16, 128, 128], P('amp', 'int'), may hold values from -0.125 to 0.125
- hole_int: bfloat16 [1024, 1024], replicated, may hold values from -0.1875 to 0.1875
- send_list: int32 [64, 64, 1], P('amp'), may hold values from 0 to 7, as said below
- slot_of: int32 [512, 16], P('amp'), may hold values from 0 to 63, as said below
Outputs:
- residual: bfloat16 [512, 1024, 128], P('amp', 'int')
Inputs may be any that keep to these rules, and one draw needn't show every extreme that they name: `send_list`: every local tile index appears in each source device's row. `slot_of`: every slot is named by some tile of each owning device.
All inputs are finite; a program needn't handle non-finite values.
Results may differ from a plain program's by a relative error of at most 0.009.
Values may be sent and summed in bfloat16 or wider, within the bound.
A program may use at most 64 MiB of HBM per device.

v0:
```python
import jax
import jax.numpy as jnp
from jax import lax
from jax.sharding import PartitionSpec as P


def body(amps, integrals, hole_int, send_list, slot_of):
    n_amp = lax.axis_size("amp")
    blk, occ_dev, width = amps.shape
    cap = send_list.shape[2]
    picks = send_list.reshape(-1)
    outgoing = jnp.take(amps, picks, axis=0).reshape(n_amp, cap, occ_dev, width)
    arrived = lax.all_to_all(outgoing, "amp", split_axis=0, concat_axis=0, tiled=True)
    arrived = arrived.reshape(n_amp * cap, occ_dev, width)
    sources = jnp.take(arrived, slot_of.reshape(-1), axis=0).reshape(blk, -1, occ_dev, width)
    ladder = jnp.einsum(
        "bkoc,bkcd->bod",
        sources,
        lax.all_gather(integrals, "int", axis=1, tiled=True),
        preferred_element_type=jnp.float32,
    )
    first = lax.axis_index("int") * occ_dev
    own_rows = lax.dynamic_slice_in_dim(hole_int, first, occ_dev, 0)
    holes = jnp.einsum(
        "pq,bqc->bpc",
        own_rows,
        lax.all_gather(amps, "int", axis=1, tiled=True),
        preferred_element_type=jnp.float32,
    ).astype(jnp.bfloat16)
    return (ladder + holes.astype(jnp.float32)).astype(jnp.bfloat16)


def solution(mesh):
    in_specs = (
        P("amp", "int", None),
        P("amp", "int", None, None),
        P(),
        P("amp", None, None),
        P("amp", None),
    )
    out_specs = P("amp", "int", None)
    return jax.shard_map(body, mesh=mesh, in_specs=in_specs, out_specs=out_specs, check_vma=False)
```

profile of v0, /device:TPU:1, one launch (start us, length us, event | category | flops | bytes accessed | tf_op | source)
XLA Modules:
  0.0 145.6 jit_solution(10318396009949058293)
XLA Ops:
  6.5 0.0 copy-start
  6.5 0.0 all-gather.5.cloned.1.call-start
  6.5 0.7 all-gather.5.cloned.1.call-update
  7.3 0.7 fusion.17
  7.9 0.0 copy-start.2
  7.9 3.1 %gather_fusion = bf16[64,128,128]{2,1,0:T(8,128)(2,1)} fusion(bf16[8,128,128]{2,1,0:T(8,128)(2,1)} %param.5, s32[1024]{0:T(1024)S(1)} %pad_clamp_fusion.1), kind=kCustom, calls=%fused_computation | custom fusion | bytes 4194560 | tf_op jit(solution)/shard_map/jit(_take)/gather | solution.py:12
  11.1 0.0 copy-done.2
  11.1 3.2 %bitcast_select_fusion = bf16[64,1,128,128]{3,2,1,0:T(8,128)(2,1)} fusion(bf16[64,128,128]{2,1,0:T(8,128)(2,1)} %gather_fusion, pred[64]{0:T(512)(128)(4,1)S(1)} %compare_and_fusion.1), kind=kLoop, calls=%fused_computation.5 | loop fusion | flops 1048576 | bytes 4194368 | tf_op jit(solution)/shard_map/jit(_take)/select_n | solution.py:12
  14.3 0.0 copy-start.1
  14.3 19.7 %all-to-all-start = ((bf16[64,1,128,128]{3,2,1,0:T(8,128)(2,1)}), bf16[64,1,128,128]{3,2,1,0:T(8,128)(2,1)}, u32[]{:S(2)}, u32[]{:S(2)}) async-start(bf16[64,1,128,128]{3,2,1,0:T(8,128)(2,1)} %bitcast_select_fusion), calls=%async_computation | async-start | bytes 4194304 | tf_op jit(solution)/shard_map/all_to_all | solution.py:13
  33.9 0.0 all-gather.3.cloned.1.call-start
  34.0 0.7 all-gather.3.cloned.1.call-update
  34.7 0.0 copy-done.1
  34.7 0.1 reshape.93
  34.8 13.2 %all-gather.5.cloned.1.call-done = bf16[8,1024,128]{2,1,0:T(8,128)(2,1)} async-done(((bf16[8,128,128]{2,1,0:T(8,128)(2,1)}), bf16[8,1024,128]{2,1,0:T(8,128)(2,1)}) %all-gather.5.cloned.1.call-update) | async-done | bytes 2097168 | tf_op jit(solution)/shard_map/all_gather | solution.py:27
  48.1 0.0 copy-done
  48.1 2.0 %fusion.14 = f32[8,128,128]{2,1,0:T(8,128)S(1)} fusion(bf16[8,1024,128]{2,1,0:T(8,128)(2,1)} %all-gather.5.cloned.1.call-done, bf16[1024,1024]{1,0:T(8,128)(2,1)S(1)} %copy-done, s32[]{:T(128)S(6)} %select_n.58), kind=kOutput, calls=%fused_computation.12 | convolution fusion | flops 268697600 | bytes 2883588 | tf_op jit(solution)/shard_map/pq,bqc->bpc/dot_general | solution.py:24
  50.1 78.5 %all-to-all-done = bf16[64,1,128,128]{3,2,1,0:T(8,128)(2,1)} async-done(((bf16[64,1,128,128]{3,2,1,0:T(8,128)(2,1)}), bf16[64,1,128,128]{3,2,1,0:T(8,128)(2,1)}, u32[]{:S(2)}, u32[]{:S(2)}) %all-to-all-start) | async-done | bytes 2097184 | tf_op jit(solution)/shard_map/all_to_all | solution.py:13
  128.6 4.6 %gather_fusion.1 = bf16[128,128,128]{2,1,0:T(8,128)(2,1)} fusion(bf16[64,128,128]{2,1,0:T(8,128)(2,1)} %bitcast.4, s32[1024]{0:T(1024)S(1)} %pad_clamp_fusion), kind=kCustom, calls=%fused_computation.1 | custom fusion | bytes 8389120 | tf_op jit(solution)/shard_map/jit(_take)/gather | solution.py:15
  133.3 0.0 all-gather.3.cloned.1.call-done
  133.3 5.5 %fusion.10 = bf16[8,128,128]{2,1,0:T(8,128)(2,1)} fusion(f32[8,128,128]{2,1,0:T(8,128)S(1)} %fusion.14, bf16[8,16,128,128]{3,2,1,0:T(8,128)(2,1)} %all-gather.3.cloned.1.call-done, bf16[8,16,128,128]{3,2,1,0:T(8,128)(2,1)} %bitcast.26, pred[8,16]{1,0:T(8,128)(4,1)S(1)} %compare_and_fusion), kind=kOutput, calls=%fused_computation.9 | convolution fusion | flops 539230208 | bytes 9175168 | tf_op jit(solution)/shard_map/bkoc,bkcd->bod/dot_general | solution.py:16
  (5 shorter events, 0.0 us)
Async XLA Ops:
  6.5 41.5 %copy-start = (bf16[1024,1024]{1,0:T(8,128)(2,1)S(1)}, bf16[1024,1024]{1,0:T(8,128)(2,1)}, u32[]{:S(2)}) copy-start(bf16[1024,1024]{1,0:T(8,128)(2,1)} %param.7) | copy-start | bytes 6291460
  6.5 41.5 %all-gather.5.cloned.1.call-start = ((), (), s32[]{:S(2)}) async-start(), calls=%async_computation.2 | async-start | bytes 2359296 | tf_op jit(solution)/shard_map/all_gather | solution.py:27
  7.9 3.1 %copy-start.2 = (s32[1,64,1]{1,2,0:T(1,128)S(1)}, s32[1,64,1]{1,2,0:T(1,128)}, u32[]{:S(2)}) copy-start(s32[1,64,1]{1,2,0:T(1,128)} %param.8) | copy-start | bytes 772
  14.3 20.4 %copy-start.1 = (s32[8,16]{1,0:T(8,128)S(1)}, s32[8,16]{1,0:T(8,128)}, u32[]{:S(2)}) copy-start(s32[8,16]{1,0:T(8,128)} %param.9) | copy-start | bytes 1540
  14.3 114.4 %all-to-all-start = ((bf16[64,1,128,128]{3,2,1,0:T(8,128)(2,1)}), bf16[64,1,128,128]{3,2,1,0:T(8,128)(2,1)}, u32[]{:S(2)}, u32[]{:S(2)}) async-start(bf16[64,1,128,128]{3,2,1,0:T(8,128)(2,1)} %bitcast_select_fusion), calls=%async_computation | async-start | bytes 4194304 | tf_op jit(solution)/shard_map/all_to_all | solution.py:13
  33.9 99.3 %all-gather.3.cloned.1.call-start = ((), (), s32[]{:S(2)}) async-start(), calls=%async_computation.1 | async-start | bytes 4718592 | tf_op jit(solution)/shard_map/all_gather | solution.py:19
Sparse Core Ops, SparseCore 0:
  9.5 38.5 all-gather.4
  50.2 40.1 all-gather.2
where the time goes:
time: 149 us; the launch traced here: 146 us
  waiting for transfers between devices  93.2 us (63%)
  starting transfers between devices  19.7 us (13%)
  between operations  13.4 us (9%)
  local copies, waits for them, and re-layouts  7.85 us (5%)
  matrix products  7.52 us (5%)
  other arithmetic  3.89 us (3%)
    all_to_all x1, waiting for transfers between devices, body(): lax.all_to_all(outgoing, 'amp', split_axis=0, concat_axis=0, tiled=True)  78.5 us
    all_to_all x1, starting transfers between devices, body(): lax.all_to_all(outgoing, 'amp', split_axis=0, concat_axis=0, tiled=True)  19.7 us
    all_gather x1, waiting for transfers between devices, body(): lax.all_gather(amps, 'int', axis=1, tiled=True)  13.2 us
    dot_general x1, matrix products, body(): jnp.einsum('bkoc,bkcd->bod', sources, lax.all_gather(integrals, 'int', ax...  5.49 us
    gather x1, local copies, waits for them, and re-layouts, body(): jnp.take(arrived, slot_of.reshape(-1), axis=0)  4.64 us
    select_n x2, other arithmetic, body(): outgoing = jnp.take(amps, picks, axis=0).reshape(n_amp, cap, occ_dev, width)  3.85 us
    gather x1, local copies, waits for them, and re-layouts, body(): outgoing = jnp.take(amps, picks, axis=0).reshape(n_amp, cap, occ_dev, width)  3.12 us
  transfers between devices with their start and end apart: 3, of which 2 were waited for; matrix products, arithmetic and copies ran while one was open for 9% of the time, Pallas kernels for 0%

commit v1 on v0

v1 whole, which is shorter than its diff:
```python
import functools

import jax
import jax.numpy as jnp
from jax import lax
from jax.experimental import pallas as pl
from jax.experimental.pallas import tpu as pltpu
from jax.sharding import PartitionSpec as P

MESH = pl.DeviceIdType.MESH
NZ = 16
CT = 2


def kernel(n_amp, n_int, amps, integrals, hole_int, row_list, slot_of, out, *scratch):
    nz = NZ
    ny = n_amp // nz
    nx = n_int // 2
    half = nz // 2
    blk = amps.shape[0]
    occ_dev = amps.shape[1]
    n_chunk = blk // CT

    scratch = list(scratch)
    plus = [amps] + scratch[: half - 1]
    minus = [amps] + scratch[half - 1 : 2 * half - 2]
    far = scratch[2 * half - 2]
    plus.append(far)
    minus.append(far)
    bufs = (plus, minus)
    (meta, meta_s, arrived, picked, all_int, all_amps, rows, held,
     zs, zr, ms, mr, ls, ys, yr, xs, xr, own_sem) = scratch[2 * half - 1 :]

    amp = lax.axis_index("amp")
    me = lax.axis_index("int")
    y, z = amp // nz, amp % nz
    x, core = me // 2, me % 2

    def at_z(shift):
        return y * nz + (z + shift + nz) % nz

    def at_y(shift):
        return ((y + shift) % ny) * nz + z

    def at_x(shift, other=0):
        side = 1 - core if other else core
        return ((x + shift + nx) % nx) * 2 + side

    z_dev = ({"amp": at_z(1)}, {"amp": at_z(-1)})
    partners = list(z_dev)
    partners += [{"amp": at_y(j)} for j in range(1, ny)]
    partners += [{"int": at_x(1)}, {"int": at_x(-1)}, {"int": at_x(0, 1)}]

    own = [
        pltpu.make_async_copy(integrals, all_int.at[me], own_sem.at[0]),
        pltpu.make_async_copy(amps, all_amps.at[me], own_sem.at[1]),
        pltpu.make_async_copy(
            hole_int.at[pl.ds(pl.multiple_of(me * occ_dev, occ_dev), occ_dev)], rows, own_sem.at[2]
        ),
        pltpu.make_async_copy(row_list, meta_s.at[0, 0], own_sem.at[3]),
    ]
    for copy in own:
        copy.start()

    barrier = pltpu.get_barrier_semaphore()
    for partner in partners:
        pl.semaphore_signal(barrier, inc=1, device_id=partner, device_id_type=MESH)
    pl.semaphore_wait(barrier, len(partners))

    sent = []

    def z_copy(d, s, c):
        part = pl.ds(c * CT, CT)
        return pltpu.make_async_remote_copy(
            src_ref=bufs[d][s - 1].at[part],
            dst_ref=bufs[d][s].at[part],
            send_sem=zs.at[d, s, c],
            recv_sem=zr.at[d, s, c],
            device_id=z_dev[d],
            device_id_type=MESH,
        )

    def m_copy(d, s):
        return pltpu.make_async_remote_copy(
            src_ref=row_list if s == 1 else meta.at[d, s - 1],
            dst_ref=meta.at[d, s],
            send_sem=ms.at[d, s],
            recv_sem=mr.at[d, s],
            device_id=z_dev[d],
            device_id_type=MESH,
        )

    def z_goes(d, s, c):
        return s < half or (s == half and (c < n_chunk // 2) == (d == 0))

    def m_goes(d, s):
        return s < half or (s == half and d == 0)

    def z_send(d, s, c):
        copy = z_copy(d, s, c)
        copy.start()
        sent.append(copy)

    def m_send(d, s):
        copy = m_copy(d, s)
        copy.start()
        sent.append(copy)

    def x_piece(ref, slot, p):
        n = blk // 2
        view = ref if slot is None else ref.at[slot]
        return view.at[pl.ds((p % 2) * n, n)]

    def x_copy(kind, p, slot, dev, first=False):
        ref, mine = (all_amps, amps) if p < 2 else (all_int, integrals)
        return pltpu.make_async_remote_copy(
            src_ref=x_piece(mine, None, p) if first else x_piece(ref, slot, p),
            dst_ref=x_piece(ref, slot, p),
            send_sem=xs.at[kind, p],
            recv_sem=xr.at[kind, p],
            device_id=dev,
            device_id_type=MESH,
        )

    x_right, x_left, x_sib = {"int": at_x(1)}, {"int": at_x(-1)}, {"int": at_x(0, 1)}

    def x_send(kind, p, slot, dev, first=False):
        copy = x_copy(kind, p, slot, dev, first)
        copy.start()
        sent.append(copy)

    def x_wait(kind, p, slot):
        x_copy(kind, p, slot, x_sib).wait_recv()

    def y_copy(j, k, slot, dev):
        return pltpu.make_async_remote_copy(
            src_ref=picked.at[j - 1, k],
            dst_ref=arrived.at[slot],
            send_sem=ys.at[j - 1, k],
            recv_sem=yr.at[j - 1, k],
            device_id=dev,
            device_id_type=MESH,
        )

    sources = [(0, 0)]
    for s in range(1, half):
        sources += [(0, s), (1, s)]
    sources.append((0, half))

    def z_of(d, s):
        return (z - s + nz) % nz if d == 0 else (z + s) % nz

    def y_phase(k):
        d, s = sources[k]
        buf = bufs[d][s]
        if s == 0:
            own[3].wait()
        else:
            to_smem = pltpu.make_async_copy(meta.at[d, s], meta_s.at[d, s], ls.at[d, s])
            to_smem.start()
            to_smem.wait()
        src_z = z_of(d, s)
        for j in range(1, ny):
            tile = meta_s[d, s, 0, at_y(j)]
            picked[j - 1, k] = buf[tile]
            copy = y_copy(j, k, y * nz + src_z, {"amp": at_y(j)})
            copy.start()
            sent.append(copy)
        tile = meta_s[d, s, 0, amp]
        arrived[y * nz + src_z] = buf[tile]

    for c in range(n_chunk):
        for d in range(2):
            z_send(d, 1, c)
        if c == 0:
            for d in range(2):
                m_send(d, 1)
    for p in range(4):
        x_send(0, p, me, x_right, first=True)
        x_send(1, p, me, x_left, first=True)
    for p in range(4):
        x_send(2, p, me, x_sib, first=True)

    def x_first_hop():
        for p in range(4):
            x_wait(0, p, at_x(-1))
            if p % 2 == 0:
                x_send(3, p, at_x(-1), x_right)
            x_wait(1, p, at_x(1))
            if p % 2 == 1:
                x_send(4, p, at_x(1), x_left)
        for p in range(4):
            x_send(5, p, at_x(-1), x_sib)
            x_send(6, p, at_x(1), x_sib)

    def x_second_hop():
        for p in range(4):
            x_wait(3 + p % 2, p, at_x(2))
            x_send(7, p, at_x(2), x_sib)

    def x_last():
        for p in range(4):
            x_wait(2, p, at_x(0, 1))
            x_wait(5, p, at_x(-1, 1))
            x_wait(6, p, at_x(1, 1))
            x_wait(7, p, at_x(2, 1))

    def hole_part():
        own[1].wait()
        own[2].wait()

        @pl.loop(0, blk)
        def _(b):
            right = all_amps[:, b].reshape(n_int * occ_dev, -1)
            total = jnp.dot(rows[...], right, preferred_element_type=jnp.float32)
            held[b] = total.astype(jnp.bfloat16)

    y_phase(0)
    for s in range(1, half + 1):
        for c in range(n_chunk):
            for d in range(2):
                if z_goes(d, s, c):
                    z_copy(d, s, c).wait_recv()
                    if s < half and z_goes(d, s + 1, c):
                        z_send(d, s + 1, c)
            if c == 0:
                for d in range(2):
                    if m_goes(d, s):
                        m_copy(d, s).wait_recv()
                        if s < half and m_goes(d, s + 1):
                            m_send(d, s + 1)
        for k, (d, t) in enumerate(sources):
            if t == s:
                y_phase(k)
        if s == half // 2:
            x_first_hop()
        if s == half - 2:
            x_second_hop()
        if s == half - 1:
            x_last()
            hole_part()

    own[0].wait()
    for k, (d, s) in enumerate(sources):
        for j in range(1, ny):
            slot = ((y - j + ny) % ny) * nz + z_of(d, s)
            y_copy(j, k, slot, {"amp": at_y(j)}).wait_recv()

    knz = slot_of.shape[1]
    per = knz // n_int

    @pl.loop(0, blk)
    def _(q):
        total = jnp.zeros(out.shape[1:], jnp.float32)
        for i in range(n_int):
            left = jnp.concatenate([arrived[slot_of[q, i * per + n]] for n in range(per)], axis=1)
            right = all_int[i, q].reshape(left.shape[1], -1)
            total += jnp.dot(left, right, preferred_element_type=jnp.float32)
        out[q] = (total + held[q].astype(jnp.float32)).astype(out.dtype)

    for copy in sent:
        copy.wait_send()


def body(amps, integrals, hole_int, send_list, slot_of):
    n_amp, n_int = lax.axis_size("amp"), lax.axis_size("int")
    blk, occ_dev, width = amps.shape
    half = NZ // 2
    ny = n_amp // NZ
    row_list = jnp.pad(send_list.reshape(1, -1), ((0, 0), (0, 128 - n_amp)))
    tiles = pltpu.VMEM((blk, occ_dev, width), amps.dtype)
    dma = pltpu.SemaphoreType.DMA
    n_chunk = blk // CT
    vmem, anywhere, smem = (pl.BlockSpec(memory_space=m) for m in (pltpu.VMEM, pl.ANY, pltpu.SMEM))
    scratch = [tiles] * (2 * half - 1)
    scratch += [
        pltpu.VMEM((2, half + 1, 1, 128), jnp.int32),
        pltpu.SMEM((2, half + 1, 1, 128), jnp.int32),
        pltpu.VMEM((n_amp, occ_dev, width), amps.dtype),
        pltpu.VMEM((ny - 1, NZ, occ_dev, width), amps.dtype),
        pltpu.VMEM((n_int,) + integrals.shape, integrals.dtype),
        pltpu.VMEM((n_int,) + amps.shape, amps.dtype),
        pltpu.VMEM((occ_dev, hole_int.shape[1]), hole_int.dtype),
        pltpu.VMEM(amps.shape, amps.dtype),
        dma((2, half + 1, n_chunk)),
        dma((2, half + 1, n_chunk)),
        dma((2, half + 1)),
        dma((2, half + 1)),
        dma((2, half + 1)),
        dma((ny - 1, NZ)),
        dma((ny - 1, NZ)),
        dma((8, 4)),
        dma((8, 4)),
        dma((4,)),
    ]
    return pl.pallas_call(
        functools.partial(kernel, n_amp, n_int),
        out_shape=jax.ShapeDtypeStruct(amps.shape, amps.dtype),
        in_specs=[vmem, anywhere, anywhere, vmem, smem],
        out_specs=vmem,
        scratch_shapes=scratch,
        compiler_params=pltpu.CompilerParams(
            collective_id=0, has_side_effects=True, vmem_limit_bytes=40 * 1024 * 1024
        ),
    )(amps, integrals, hole_int, row_list, slot_of)


def solution(mesh):
    in_specs = (
        P("amp", "int", None),
        P("amp", "int", None, None),
        P(),
        P("amp", None, None),
        P("amp", None),
    )
    out_specs = P("amp", "int", None)
    return jax.shard_map(body, mesh=mesh, in_specs=in_specs, out_specs=out_specs, check_vma=False)
```

time: 149 us -> 74.1 us (0.50); the launches traced: 146 us -> 73.8 us
  waiting for transfers between devices: 93.2 us -> 0 us
  Pallas kernels: 0 us -> 68.1 us
  starting transfers between devices: 19.7 us -> 0 us
  between operations: 13.4 us -> 0.01 us
  matrix products: 7.52 us -> 0 us
  other arithmetic: 3.89 us -> 0 us
  local copies, waits for them, and re-layouts: 7.85 us -> 5.63 us
    all_to_all x1 -> x0, waiting for transfers between devices: 78.5 us -> none  [body(): lax.all_to_all(outgoing, 'amp', split_axis=0, concat_axis=0, tiled=True)]
    pallas_call x0 -> x1, Pallas kernels: none -> 68.1 us  [body(): pl.pallas_call(functools.partial(kernel, n_amp, n_int), out_shape=jax.Sha...]
    all_to_all x1 -> x0, starting transfers between devices: 19.7 us -> none  [body(): lax.all_to_all(outgoing, 'amp', split_axis=0, concat_axis=0, tiled=True)]
    all_gather x2 -> x0, waiting for transfers between devices: 13.2 us -> none  [the longest x1 13.2 us: body(): lax.all_gather(amps, 'int', axis=1, tiled=True)]
    gather x2 -> x0, local copies, waits for them, and re-layouts: 7.76 us -> none  [the longest x1 4.64 us: body(): jnp.take(arrived, slot_of.reshape(-1), axis=0)]
    dot_general x2 -> x0, matrix products: 7.52 us -> none  [the longest x1 5.49 us: body(): jnp.einsum('bkoc,bkcd->bod', sources, lax.all_gather(integrals, 'int', ax...]
    unnamed x6 -> x9, local copies, waits for them, and re-layouts: 0.01 us -> 4.97 us
    select_n x3 -> x0, other arithmetic: 3.86 us -> none  [the longest x2 3.85 us: body(): outgoing = jnp.take(amps, picks, axis=0).reshape(n_amp, cap, occ_dev, width)]
  transfers between devices with their start and end apart: 3 -> 0, of which waited for: 2 -> 0; matrix products, arithmetic and copies ran while one was open for 9% -> 0% of each run, Pallas kernels for 0% -> 0%
where the time goes in v1:
time: 74.1 us; the launch traced here: 73.8 us
  Pallas kernels  68.1 us (92%)
  local copies, waits for them, and re-layouts  5.63 us (8%)
    pallas_call x1, Pallas kernels, body(): pl.pallas_call(functools.partial(kernel, n_amp, n_int), out_shape=jax.Sha...  68.1 us
    unnamed x9, local copies, waits for them, and re-layouts  4.97 us

profile of v1, /device:TPU:1, one launch (start us, length us, event | category | flops | bytes accessed | tf_op | source)
XLA Modules:
  0.0 73.8 jit_solution(6063007815199230868)
XLA Ops:
  0.0 0.7 pad.4.row_list
  0.7 0.0 copy-start
  0.7 1.6 %copy-done = bf16[1024,1024]{1,0:T(8,128)(2,1)S(1)} copy-done((bf16[1024,1024]{1,0:T(8,128)(2,1)S(1)}, bf16[1024,1024]{1,0:T(8,128)(2,1)}, u32[]{:S(2)}) %copy-start) | copy-done | bytes 2097176
  2.3 0.0 copy-start.1
  2.3 1.0 %copy-done.1 = bf16[8,2,128,128]{3,2,1,0:T(8,128)(2,1)S(1)} copy-done((bf16[8,2,128,128]{3,2,1,0:T(8,128)(2,1)S(1)}, bf16[8,2,128,128]{3,2,1,0:T(8,128)(2,1)}, u32[]{:S(2)}) %copy-start.1) | copy-done | bytes 524312
  3.3 0.0 copy-start.2
  3.3 0.9 %copy-done.2 = bf16[8,128,128]{2,1,0:T(8,128)(2,1)S(1)} copy-done((bf16[8,128,128]{2,1,0:T(8,128)(2,1)S(1)}, bf16[8,128,128]{2,1,0:T(8,128)(2,1)}, u32[]{:S(2)}) %copy-start.2) | copy-done | bytes 262168
  4.2 0.0 copy-start.3
  4.2 0.7 copy-done.3
  4.9 68.1 %shard_map.55 = bf16[8,128,128]{2,1,0:T(8,128)(2,1)S(1)} custom-call(bf16[8,128,128]{2,1,0:T(8,128)(2,1)S(1)} %copy-done.2, bf16[8,2,128,128]{3,2,1,0:T(8,128)(2,1)S(1)} %copy-done.1, bf16[1024,1024]{1,0:T(8,128)(2,1)S(1)} %copy-done, s32[1,128]{1,0:T(1,128)S(1)} %pad.4.row_list, s32[8,16]{1,0:T(8,128)S(1)} %copy-done.3), custom_call_target="tpu_custom_call" | custom-call | tf_op jit(solution)/shard_map/pallas_call | solution.py:296
  73.1 0.7 copy.7
Async XLA Ops:
  0.7 1.6 %copy-start = (bf16[1024,1024]{1,0:T(8,128)(2,1)S(1)}, bf16[1024,1024]{1,0:T(8,128)(2,1)}, u32[]{:S(2)}) copy-start(bf16[1024,1024]{1,0:T(8,128)(2,1)} %hole_int.1) | copy-start | bytes 6291460
  2.3 1.0 %copy-start.1 = (bf16[8,2,128,128]{3,2,1,0:T(8,128)(2,1)S(1)}, bf16[8,2,128,128]{3,2,1,0:T(8,128)(2,1)}, u32[]{:S(2)}) copy-start(bf16[8,2,128,128]{3,2,1,0:T(8,128)(2,1)} %integrals.1) | copy-start | bytes 1572868
  3.3 0.9 %copy-start.2 = (bf16[8,128,128]{2,1,0:T(8,128)(2,1)S(1)}, bf16[8,128,128]{2,1,0:T(8,128)(2,1)}, u32[]{:S(2)}) copy-start(bf16[8,128,128]{2,1,0:T(8,128)(2,1)} %amps.1) | copy-start | bytes 786436
  4.2 0.7 copy-start.3

commit v2 on v1

v2 whole, which is shorter than its diff:
```python
import functools

import jax
import jax.numpy as jnp
from jax import lax
from jax.experimental import pallas as pl
from jax.experimental.pallas import tpu as pltpu
from jax.sharding import PartitionSpec as P

MESH = pl.DeviceIdType.MESH
NZ = 16
CT = 2


def kernel(n_amp, n_int, amps, integrals, hole_int, row_list, slot_list, out, *scratch):
    nz = NZ
    ny = n_amp // nz
    nx = n_int // 2
    half = nz // 2
    blk = amps.shape[0]
    occ_dev = amps.shape[1]
    n_chunk = blk // CT

    scratch = list(scratch)
    reach = half - 2
    plus = [amps] + scratch[:reach]
    minus = [amps] + scratch[reach : 2 * reach]
    bufs = (plus, minus)
    (mine, meta, meta_s, slot_of, arrived, picked, all_int, all_amps, rows, held, result,
     zs, zr, ms, mr, ls, ys, yr, xs, xr, own_sem, out_sem) = scratch[2 * reach :]

    amp = lax.axis_index("amp")
    me = lax.axis_index("int")
    y, z = amp // nz, amp % nz
    x, core = me // 2, me % 2

    def at_z(shift):
        return y * nz + (z + shift + nz) % nz

    def at_y(shift):
        return ((y + shift) % ny) * nz + z

    def at_x(shift, other=0):
        side = 1 - core if other else core
        return ((x + shift + nx) % nx) * 2 + side

    z_dev = ({"amp": at_z(1)}, {"amp": at_z(-1)})
    partners = list(z_dev)
    partners += [{"amp": at_y(j)} for j in range(1, ny)]
    partners += [{"int": at_x(1)}, {"int": at_x(-1)}, {"int": at_x(0, 1)}]

    own = [
        pltpu.make_async_copy(integrals, all_int.at[me], own_sem.at[0]),
        pltpu.make_async_copy(amps, all_amps.at[me], own_sem.at[1]),
        pltpu.make_async_copy(
            hole_int.at[pl.ds(pl.multiple_of(me * occ_dev, occ_dev), occ_dev)], rows, own_sem.at[2]
        ),
        pltpu.make_async_copy(row_list, meta_s.at[0, 0], own_sem.at[3]),
        pltpu.make_async_copy(slot_list, slot_of, own_sem.at[4]),
        pltpu.make_async_copy(amps, mine, own_sem.at[5]),
    ]
    for copy in own:
        copy.start()

    barrier = pltpu.get_barrier_semaphore()
    for partner in partners:
        pl.semaphore_signal(barrier, inc=1, device_id=partner, device_id_type=MESH)
    pl.semaphore_wait(barrier, len(partners))

    sent = []

    def z_copy(d, s, c):
        part = pl.ds(c * CT, CT)
        return pltpu.make_async_remote_copy(
            src_ref=bufs[d][s - 1].at[part],
            dst_ref=bufs[d][s].at[part],
            send_sem=zs.at[d, s, c],
            recv_sem=zr.at[d, s, c],
            device_id=z_dev[d],
            device_id_type=MESH,
        )

    def m_copy(d, s):
        return pltpu.make_async_remote_copy(
            src_ref=row_list if s == 1 else meta.at[d, s - 1],
            dst_ref=meta.at[d, s],
            send_sem=ms.at[d, s],
            recv_sem=mr.at[d, s],
            device_id=z_dev[d],
            device_id_type=MESH,
        )

    def z_send(d, s, c):
        copy = z_copy(d, s, c)
        copy.start()
        sent.append(copy)

    def m_send(d, s):
        copy = m_copy(d, s)
        copy.start()
        sent.append(copy)

    def x_piece(ref, slot, p):
        n = blk // 2
        view = ref if slot is None else ref.at[slot]
        return view.at[pl.ds((p % 2) * n, n)]

    def x_copy(kind, p, slot, dev, first=False):
        ref, mine = (all_amps, amps) if p < 2 else (all_int, integrals)
        return pltpu.make_async_remote_copy(
            src_ref=x_piece(mine, None, p) if first else x_piece(ref, slot, p),
            dst_ref=x_piece(ref, slot, p),
            send_sem=xs.at[kind, p],
            recv_sem=xr.at[kind, p],
            device_id=dev,
            device_id_type=MESH,
        )

    x_right, x_left, x_sib = {"int": at_x(1)}, {"int": at_x(-1)}, {"int": at_x(0, 1)}

    def x_send(kind, p, slot, dev, first=False):
        copy = x_copy(kind, p, slot, dev, first)
        copy.start()
        sent.append(copy)

    def x_wait(kind, p, slot):
        x_copy(kind, p, slot, x_sib).wait_recv()

    named = []
    near = {}
    for d, t in [(0, 0)] + [(d, t) for t in range(1, reach + 1) for d in range(2)]:
        near[d, t] = range(len(named), len(named) + ny - 1)
        named += [(d, t, j, 0) for j in range(1, ny)]
    beyond = []
    for n in range(ny // 2):
        for d in range(2):
            beyond.append(len(named))
            named.append((d, reach, n + d * (ny // 2), 2 - 4 * d))
    for j in (ny // 2, *range(1, ny // 2), *range(ny // 2 + 1, ny), 0):
        for d in range(2):
            beyond.append(len(named))
            named.append((d, reach, j, 1 - 2 * d))

    def z_of(d, t, shift):
        return (z + shift + (t if d else -t) + nz) % nz

    def n_copy(n, dev, slot):
        return pltpu.make_async_remote_copy(
            src_ref=picked.at[n],
            dst_ref=arrived.at[slot],
            send_sem=ys.at[n],
            recv_sem=yr.at[n],
            device_id=dev,
            device_id_type=MESH,
        )

    def tile_for(d, t, target):
        buf = bufs[d][t] if t else mine
        return buf[meta_s[d, t, 0, target]]

    def n_send(n):
        d, t, j, shift = named[n]
        target = ((y + j) % ny) * nz + (z + shift + nz) % nz
        picked[n] = tile_for(d, t, target)
        copy = n_copy(n, {"amp": target}, y * nz + z_of(d, t, 0))
        copy.start()
        sent.append(copy)

    def n_wait(n):
        d, t, j, shift = named[n]
        slot = ((y - j + ny) % ny) * nz + z_of(d, t, -shift)
        n_copy(n, {"amp": at_y(1)}, slot).wait_recv()

    def to_smem(d, t):
        return pltpu.make_async_copy(meta.at[d, t], meta_s.at[d, t], ls.at[d, t])

    def keep_own(d, t):
        arrived[y * nz + z_of(d, t, 0)] = tile_for(d, t, amp)

    def name_part(t, part):
        for d in range(2):
            if part == 0:
                to_smem(d, t).wait()
            if part < ny - 1:
                n_send(near[d, t][part])
            else:
                keep_own(d, t)

    for c in range(n_chunk):
        for d in range(2):
            z_send(d, 1, c)
        if c == 0:
            for d in range(2):
                m_send(d, 1)
    for p, r in ((2, 3), (0, 1), (3, 2), (1, 0)):
        x_send(0, p, me, x_right, first=True)
        x_send(1, r, me, x_left, first=True)
    for p in range(4):
        x_send(2, p, me, x_sib, first=True)

    def x_stage(stage):
        if stage == 0:
            for p in (2, 0):
                x_wait(0, p, at_x(-1))
                x_send(3, p, at_x(-1), x_right)
                x_wait(1, p + 1, at_x(1))
                x_send(4, p + 1, at_x(1), x_left)
        elif stage == 1:
            for p in (3, 1):
                x_wait(0, p, at_x(-1))
                x_wait(1, p - 1, at_x(1))
            for p in range(4):
                x_send(5, p, at_x(-1), x_sib)
                x_send(6, p, at_x(1), x_sib)
        elif stage == 2:
            for p in range(4):
                x_wait(3 + p % 2, p, at_x(2))
                x_send(7, p, at_x(2), x_sib)
        else:
            for p in range(4):
                x_wait(2, p, at_x(0, 1))
                x_wait(5, p, at_x(-1, 1))
                x_wait(6, p, at_x(1, 1))
                x_wait(7, p, at_x(2, 1))

    def hole_part():
        own[1].wait()
        own[2].wait()

        @pl.loop(0, blk)
        def _(b):
            right = all_amps[:, b].reshape(n_int * occ_dev, -1)
            total = jnp.dot(rows[...], right, preferred_element_type=jnp.float32)
            held[b] = total.astype(jnp.bfloat16)

    own[3].wait()
    own[5].wait()
    for n in near[0, 0]:
        n_send(n)
    keep_own(0, 0)
    for t in range(1, reach + 1):
        for c in range(n_chunk):
            for d in range(2):
                z_copy(d, t, c).wait_recv()
                if t < reach:
                    z_send(d, t + 1, c)
            if c == 0:
                for d in range(2):
                    m_copy(d, t).wait_recv()
                    if t < reach:
                        m_send(d, t + 1)
                    to_smem(d, t).start()
            if t > 1:
                name_part(t - 1, c)
        if t >= reach - 3 and t < reach:
            x_stage(t - reach + 3)
    for d in range(2):
        to_smem(d, reach).wait()
    for n in beyond:
        n_send(n)
    for i in range(ny - 1):
        for d in range(2):
            n_send(near[d, reach][i])
    for d in range(2):
        keep_own(d, reach)
    x_stage(3)
    hole_part()

    own[0].wait()
    own[4].wait()
    for n in range(len(named)):
        n_wait(n)

    knz = slot_of.shape[1]
    per = knz // n_int

    def finish(q):
        return pltpu.make_async_copy(result.at[q], out.at[q], out_sem.at[q])

    for q in range(blk):
        total = jnp.zeros(out.shape[1:], jnp.float32)
        for i in range(n_int):
            left = jnp.concatenate([arrived[slot_of[q, i * per + n]] for n in range(per)], axis=1)
            right = all_int[i, q].reshape(left.shape[1], -1)
            total += jnp.dot(left, right, preferred_element_type=jnp.float32)
        result[q] = (total + held[q].astype(jnp.float32)).astype(out.dtype)
        finish(q).start()

    for copy in sent:
        copy.wait_send()
    for q in range(blk):
        finish(q).wait()


def body(amps, integrals, hole_int, send_list, slot_of):
    n_amp, n_int = lax.axis_size("amp"), lax.axis_size("int")
    blk, occ_dev, width = amps.shape
    half = NZ // 2
    ny = n_amp // NZ
    row_list = send_list.reshape(1, n_amp)
    tiles = pltpu.VMEM((blk, occ_dev, width), amps.dtype)
    dma = pltpu.SemaphoreType.DMA
    n_chunk = blk // CT
    hbm = pl.BlockSpec(memory_space=pltpu.HBM)
    reach = half - 2
    n_named = (2 * reach + 1) * (ny - 1) + 3 * ny
    scratch = [tiles] * (2 * reach)
    scratch += [
        tiles,
        pltpu.VMEM((2, reach + 1, 1, n_amp), jnp.int32),
        pltpu.SMEM((2, reach + 1, 1, n_amp), jnp.int32),
        pltpu.SMEM(slot_of.shape, jnp.int32),
        pltpu.VMEM((n_amp, occ_dev, width), amps.dtype),
        pltpu.VMEM((n_named, occ_dev, width), amps.dtype),
        pltpu.VMEM((n_int,) + integrals.shape, integrals.dtype),
        pltpu.VMEM((n_int,) + amps.shape, amps.dtype),
        pltpu.VMEM((occ_dev, hole_int.shape[1]), hole_int.dtype),
        tiles,
        tiles,
        dma((2, reach + 1, n_chunk)),
        dma((2, reach + 1, n_chunk)),
        dma((2, reach + 1)),
        dma((2, reach + 1)),
        dma((2, reach + 1)),
        dma((n_named,)),
        dma((n_named,)),
        dma((8, 4)),
        dma((8, 4)),
        dma((6,)),
        dma((blk,)),
    ]
    return pl.pallas_call(
        functools.partial(kernel, n_amp, n_int),
        out_shape=jax.ShapeDtypeStruct(amps.shape, amps.dtype),
        in_specs=[hbm] * 5,
        out_specs=hbm,
        scratch_shapes=scratch,
        compiler_params=pltpu.CompilerParams(
            collective_id=0, has_side_effects=True, vmem_limit_bytes=56 * 1024 * 1024
        ),
    )(amps, integrals, hole_int, row_list, slot_of)


def solution(mesh):
    in_specs = (
        P("amp", "int", None),
        P("amp", "int", None, None),
        P(),
        P("amp", None, None),
        P("amp", None),
    )
    out_specs = P("amp", "int", None)
    return jax.shard_map(body, mesh=mesh, in_specs=in_specs, out_specs=out_specs, check_vma=False)
```

time: 74.1 us -> 64.1 us (0.87)
  Pallas kernels: 68.1 us -> 62.3 us
  local copies, waits for them, and re-layouts: 5.63 us -> 1.67 us
    pallas_call x1, Pallas kernels: 68.1 us -> 62.3 us  [body(): pl.pallas_call(functools.partial(kernel, n_amp, n_int), out_shape=jax.Sha...]
    unnamed x9 -> x1, local copies, waits for them, and re-layouts: 4.97 us -> 1.67 us
where the time goes in v2:
time: 64.1 us; the launch traced here: 64 us
  Pallas kernels  62.3 us (97%)
  local copies, waits for them, and re-layouts  1.67 us (3%)
    pallas_call x1, Pallas kernels, body(): pl.pallas_call(functools.partial(kernel, n_amp, n_int), out_shape=jax.Sha...  62.3 us
    unnamed x1, local copies, waits for them, and re-layouts  1.67 us

profile of v2, /device:TPU:1, one launch (start us, length us, event | category | flops | bytes accessed | tf_op | source)
XLA Modules:
  0.0 64.0 jit_solution(4951397718465986345)
XLA Ops:
  0.0 62.3 %shard_map.55 = bf16[8,128,128]{2,1,0:T(8,128)(2,1)} custom-call(bf16[8,128,128]{2,1,0:T(8,128)(2,1)} %amps.1, bf16[8,2,128,128]{3,2,1,0:T(8,128)(2,1)} %integrals.1, bf16[1024,1024]{1,0:T(8,128)(2,1)} %hole_int.1, s32[1,64]{1,0:T(1,128)} %bitcast.1, s32[8,16]{1,0:T(8,128)} %slot_list.1), custom_call_target="tpu_custom_call" | custom-call | tf_op jit(solution)/shard_map/pallas_call | solution.py:332
  62.3 1.7 %copy.7 = bf16[8,128,128]{2,1,0:T(8,128)(2,1)} copy(bf16[8,128,128]{2,1,0:T(8,128)(2,1)} %shard_map.55) | data formatting | bytes 524288

commit v3 on v2

--- a/solution.py
+++ b/solution.py
@@ -10,6 +10,7 @@
 MESH = pl.DeviceIdType.MESH
 NZ = 16
 CT = 2
+STAGE = ((0, 1, 0, 1), (1, 0, 1, 0), (3,) * 4, (2,) * 4, (2,) * 4, (3,) * 4, (3,) * 4, (3,) * 4)
 
 
 def kernel(n_amp, n_int, amps, integrals, hole_int, row_list, slot_list, out, *scratch):
@@ -67,15 +68,16 @@
         pl.semaphore_signal(barrier, inc=1, device_id=partner, device_id_type=MESH)
     pl.semaphore_wait(barrier, len(partners))
 
-    sent = []
+    def arrival(ref, sem):
+        pltpu.make_async_copy(ref, ref, sem).wait()
 
     def z_copy(d, s, c):
         part = pl.ds(c * CT, CT)
         return pltpu.make_async_remote_copy(
             src_ref=bufs[d][s - 1].at[part],
             dst_ref=bufs[d][s].at[part],
-            send_sem=zs.at[d, s, c],
-            recv_sem=zr.at[d, s, c],
+            send_sem=zs,
+            recv_sem=zr.at[d, s - 1, c],
             device_id=z_dev[d],
             device_id_type=MESH,
         )
@@ -84,8 +86,8 @@
         return pltpu.make_async_remote_copy(
             src_ref=row_list if s == 1 else meta.at[d, s - 1],
             dst_ref=meta.at[d, s],
-            send_sem=ms.at[d, s],
-            recv_sem=mr.at[d, s],
+            send_sem=ms,
+            recv_sem=mr.at[d, s - 1],
             device_id=z_dev[d],
             device_id_type=MESH,
         )
@@ -93,12 +95,10 @@
     def z_send(d, s, c):
         copy = z_copy(d, s, c)
         copy.start()
-        sent.append(copy)
 
     def m_send(d, s):
         copy = m_copy(d, s)
         copy.start()
-        sent.append(copy)
 
     def x_piece(ref, slot, p):
         n = blk // 2
@@ -110,8 +110,8 @@
         return pltpu.make_async_remote_copy(
             src_ref=x_piece(mine, None, p) if first else x_piece(ref, slot, p),
             dst_ref=x_piece(ref, slot, p),
-            send_sem=xs.at[kind, p],
-            recv_sem=xr.at[kind, p],
+            send_sem=xs.at[p // 2],
+            recv_sem=xr.at[STAGE[kind][p], p // 2],
             device_id=dev,
             device_id_type=MESH,
         )
@@ -121,10 +121,10 @@
     def x_send(kind, p, slot, dev, first=False):
         copy = x_copy(kind, p, slot, dev, first)
         copy.start()
-        sent.append(copy)
-
-    def x_wait(kind, p, slot):
-        x_copy(kind, p, slot, x_sib).wait_recv()
+
+    def x_wait(stage, n):
+        for sem, ref in ((0, all_amps), (1, all_int)):
+            arrival(ref.at[pl.ds(0, n)], xr.at[stage, sem])
 
     named = []
     near = {}
@@ -148,8 +148,8 @@
         return pltpu.make_async_remote_copy(
             src_ref=picked.at[n],
             dst_ref=arrived.at[slot],
-            send_sem=ys.at[n],
-            recv_sem=yr.at[n],
+            send_sem=ys,
+            recv_sem=yr,
             device_id=dev,
             device_id_type=MESH,
         )
@@ -164,23 +164,15 @@
         picked[n] = tile_for(d, t, target)
         copy = n_copy(n, {"amp": target}, y * nz + z_of(d, t, 0))
         copy.start()
-        sent.append(copy)
-
-    def n_wait(n):
-        d, t, j, shift = named[n]
-        slot = ((y - j + ny) % ny) * nz + z_of(d, t, -shift)
-        n_copy(n, {"amp": at_y(1)}, slot).wait_recv()
 
     def to_smem(d, t):
-        return pltpu.make_async_copy(meta.at[d, t], meta_s.at[d, t], ls.at[d, t])
+        return pltpu.make_async_copy(meta.at[d, t], meta_s.at[d, t], ls.at[d])
 
     def keep_own(d, t):
         arrived[y * nz + z_of(d, t, 0)] = tile_for(d, t, amp)
 
     def name_part(t, part):
         for d in range(2):
-            if part == 0:
-                to_smem(d, t).wait()
             if part < ny - 1:
                 n_send(near[d, t][part])
             else:
@@ -200,28 +192,21 @@
 
     def x_stage(stage):
         if stage == 0:
+            x_wait(0, 1)
             for p in (2, 0):
-                x_wait(0, p, at_x(-1))
                 x_send(3, p, at_x(-1), x_right)
-                x_wait(1, p + 1, at_x(1))
                 x_send(4, p + 1, at_x(1), x_left)
         elif stage == 1:
-            for p in (3, 1):
-                x_wait(0, p, at_x(-1))
-                x_wait(1, p - 1, at_x(1))
+            x_wait(1, 1)
             for p in range(4):
                 x_send(5, p, at_x(-1), x_sib)
                 x_send(6, p, at_x(1), x_sib)
         elif stage == 2:
+            x_wait(2, 1)
             for p in range(4):
-                x_wait(3 + p % 2, p, at_x(2))
                 x_send(7, p, at_x(2), x_sib)
         else:
-            for p in range(4):
-                x_wait(2, p, at_x(0, 1))
-                x_wait(5, p, at_x(-1, 1))
-                x_wait(6, p, at_x(1, 1))
-                x_wait(7, p, at_x(2, 1))
+            x_wait(3, n_int // 2)
 
     def hole_part():
         own[1].wait()
@@ -249,6 +234,8 @@
                     m_copy(d, t).wait_recv()
                     if t < reach:
                         m_send(d, t + 1)
+                    if t > 1:
+                        to_smem(d, t - 1).wait()
                     to_smem(d, t).start()
             if t > 1:
                 name_part(t - 1, c)
@@ -268,14 +255,13 @@
 
     own[0].wait()
     own[4].wait()
-    for n in range(len(named)):
-        n_wait(n)
+    arrival(picked, yr)
 
     knz = slot_of.shape[1]
     per = knz // n_int
 
     def finish(q):
-        return pltpu.make_async_copy(result.at[q], out.at[q], out_sem.at[q])
+        return pltpu.make_async_copy(result.at[q], out.at[q], out_sem)
 
     for q in range(blk):
         total = jnp.zeros(out.shape[1:], jnp.float32)
@@ -286,10 +272,14 @@
         result[q] = (total + held[q].astype(jnp.float32)).astype(out.dtype)
         finish(q).start()
 
-    for copy in sent:
-        copy.wait_send()
-    for q in range(blk):
-        finish(q).wait()
+    for d in range(2):
+        for t in range(1, reach + 1):
+            arrival(bufs[d][t], zs)
+    arrival(meta.at[:, pl.ds(1, reach)], ms)
+    arrival(picked, ys)
+    for sem, ref in ((0, all_amps), (1, all_int)):
+        arrival(ref.at[pl.ds(0, n_int - 1)], xs.at[sem])
+    arrival(out, out_sem)
 
 
 def body(amps, integrals, hole_int, send_list, slot_of):
@@ -317,17 +307,17 @@
         pltpu.VMEM((occ_dev, hole_int.shape[1]), hole_int.dtype),
         tiles,
         tiles,
-        dma((2, reach + 1, n_chunk)),
-        dma((2, reach + 1, n_chunk)),
-        dma((2, reach + 1)),
-        dma((2, reach + 1)),
-        dma((2, reach + 1)),
-        dma((n_named,)),
-        dma((n_named,)),
-        dma((8, 4)),
-        dma((8, 4)),
+        dma,
+        dma((2, reach, n_chunk)),
+        dma,
+        dma((2, reach)),
+        dma((2,)),
+        dma,
+        dma,
+        dma((2,)),
+        dma((4, 2)),
         dma((6,)),
-        dma((blk,)),
+        dma,
     ]
     return pl.pallas_call(
         functools.partial(kernel, n_amp, n_int),

time: 64.1 us -> 61.8 us (0.964)
  Pallas kernels: 62.3 us -> 60 us
    pallas_call x1, Pallas kernels: 62.3 us -> 60 us  [body(): pl.pallas_call(functools.partial(kernel, n_amp, n_int), out_shape=jax.Sha...]
where the time goes in v3:
time: 61.8 us; the launch traced here: 61.7 us
  Pallas kernels  60 us (97%)
  local copies, waits for them, and re-layouts  1.67 us (3%)
    pallas_call x1, Pallas kernels, body(): pl.pallas_call(functools.partial(kernel, n_amp, n_int), out_shape=jax.Sha...  60 us
    unnamed x1, local copies, waits for them, and re-layouts  1.67 us

profile of v3, /device:TPU:1, one launch (start us, length us, event | category | flops | bytes accessed | tf_op | source)
XLA Modules:
  0.0 61.7 jit_solution(7648378887858798683)
XLA Ops:
  0.0 60.0 %shard_map.55 = bf16[8,128,128]{2,1,0:T(8,128)(2,1)} custom-call(bf16[8,128,128]{2,1,0:T(8,128)(2,1)} %amps.1, bf16[8,2,128,128]{3,2,1,0:T(8,128)(2,1)} %integrals.1, bf16[1024,1024]{1,0:T(8,128)(2,1)} %hole_int.1, s32[1,64]{1,0:T(1,128)} %bitcast.1, s32[8,16]{1,0:T(8,128)} %slot_list.1), custom_call_target="tpu_custom_call" | custom-call | tf_op jit(solution)/shard_map/pallas_call | solution.py:322
  60.0 1.7 %copy.7 = bf16[8,128,128]{2,1,0:T(8,128)(2,1)} copy(bf16[8,128,128]{2,1,0:T(8,128)(2,1)} %shard_map.55) | data formatting | bytes 524288

commit v4 on v3

--- a/solution.py
+++ b/solution.py
@@ -9,6 +9,7 @@
 
 MESH = pl.DeviceIdType.MESH
 NZ = 16
+REACH = 5
 CT = 2
 STAGE = ((0, 1, 0, 1), (1, 0, 1, 0), (3,) * 4, (2,) * 4, (2,) * 4, (3,) * 4, (3,) * 4, (3,) * 4)
 
@@ -23,12 +24,12 @@
     n_chunk = blk // CT
 
     scratch = list(scratch)
-    reach = half - 2
+    reach = REACH
     plus = [amps] + scratch[:reach]
     minus = [amps] + scratch[reach : 2 * reach]
     bufs = (plus, minus)
-    (mine, meta, meta_s, slot_of, arrived, picked, all_int, all_amps, rows, held, result,
-     zs, zr, ms, mr, ls, ys, yr, xs, xr, own_sem, out_sem) = scratch[2 * reach :]
+    (mine, meta, meta_s, slot_of, arrived, picked, all_int, all_amps, rows, held,
+     zs, zr, ms, mr, ls, ys, yr, xs, xr, own_sem) = scratch[2 * reach :]
 
     amp = lax.axis_index("amp")
     me = lax.axis_index("int")
@@ -131,15 +132,13 @@
     for d, t in [(0, 0)] + [(d, t) for t in range(1, reach + 1) for d in range(2)]:
         near[d, t] = range(len(named), len(named) + ny - 1)
         named += [(d, t, j, 0) for j in range(1, ny)]
-    beyond = []
-    for n in range(ny // 2):
-        for d in range(2):
-            beyond.append(len(named))
-            named.append((d, reach, n + d * (ny // 2), 2 - 4 * d))
-    for j in (ny // 2, *range(1, ny // 2), *range(ny // 2 + 1, ny), 0):
-        for d in range(2):
-            beyond.append(len(named))
-            named.append((d, reach, j, 1 - 2 * d))
+    beyond = {}
+    for h in range(1, half - reach + 1):
+        for j in range(ny):
+            for d in range(2):
+                if reach + h < half or j // (ny // 2) == d:
+                    beyond[h, j, d] = len(named)
+                    named.append((d, reach, j, h - 2 * d * h))
 
     def z_of(d, t, shift):
         return (z + shift + (t if d else -t) + nz) % nz
@@ -243,11 +242,15 @@
             x_stage(t - reach + 3)
     for d in range(2):
         to_smem(d, reach).wait()
-    for n in beyond:
-        n_send(n)
-    for i in range(ny - 1):
+    by_y = (2, 1, 3, 0)
+    for h in range(half - reach, 0, -1):
+        for j in by_y:
+            for d in range(2):
+                if (h, j, d) in beyond:
+                    n_send(beyond[h, j, d])
+    for j in by_y[:-1]:
         for d in range(2):
-            n_send(near[d, reach][i])
+            n_send(near[d, reach][j - 1])
     for d in range(2):
         keep_own(d, reach)
     x_stage(3)
@@ -259,9 +262,6 @@
 
     knz = slot_of.shape[1]
     per = knz // n_int
-
-    def finish(q):
-        return pltpu.make_async_copy(result.at[q], out.at[q], out_sem)
 
     for q in range(blk):
         total = jnp.zeros(out.shape[1:], jnp.float32)
@@ -269,8 +269,7 @@
             left = jnp.concatenate([arrived[slot_of[q, i * per + n]] for n in range(per)], axis=1)
             right = all_int[i, q].reshape(left.shape[1], -1)
             total += jnp.dot(left, right, preferred_element_type=jnp.float32)
-        result[q] = (total + held[q].astype(jnp.float32)).astype(out.dtype)
-        finish(q).start()
+        out[q] = (total + held[q].astype(jnp.float32)).astype(out.dtype)
 
     for d in range(2):
         for t in range(1, reach + 1):
@@ -279,7 +278,6 @@
     arrival(picked, ys)
     for sem, ref in ((0, all_amps), (1, all_int)):
         arrival(ref.at[pl.ds(0, n_int - 1)], xs.at[sem])
-    arrival(out, out_sem)
 
 
 def body(amps, integrals, hole_int, send_list, slot_of):
@@ -292,8 +290,9 @@
     dma = pltpu.SemaphoreType.DMA
     n_chunk = blk // CT
     hbm = pl.BlockSpec(memory_space=pltpu.HBM)
-    reach = half - 2
-    n_named = (2 * reach + 1) * (ny - 1) + 3 * ny
+    operands = (amps, integrals, hole_int, row_list, slot_of)
+    reach = REACH
+    n_named = (2 * reach + 1) * (ny - 1) + (2 * (half - reach) - 1) * ny
     scratch = [tiles] * (2 * reach)
     scratch += [
         tiles,
@@ -306,7 +305,6 @@
         pltpu.VMEM((n_int,) + amps.shape, amps.dtype),
         pltpu.VMEM((occ_dev, hole_int.shape[1]), hole_int.dtype),
         tiles,
-        tiles,
         dma,
         dma((2, reach, n_chunk)),
         dma,
@@ -317,18 +315,17 @@
         dma((2,)),
         dma((4, 2)),
         dma((6,)),
-        dma,
     ]
     return pl.pallas_call(
         functools.partial(kernel, n_amp, n_int),
         out_shape=jax.ShapeDtypeStruct(amps.shape, amps.dtype),
-        in_specs=[hbm] * 5,
-        out_specs=hbm,
+        in_specs=[hbm] * len(operands),
+        out_specs=pl.BlockSpec(memory_space=pltpu.VMEM),
         scratch_shapes=scratch,
         compiler_params=pltpu.CompilerParams(
-            collective_id=0, has_side_effects=True, vmem_limit_bytes=56 * 1024 * 1024
+            collective_id=0, has_side_effects=True, vmem_limit_bytes=48 * 1024 * 1024
         ),
-    )(amps, integrals, hole_int, row_list, slot_of)
+    )(*(pltpu.with_memory_space_constraint(a, pltpu.HBM) for a in operands))
 
 
 def solution(mesh):

time: 61.8 us -> 59.2 us (0.958)
  Pallas kernels: 60 us -> 58.4 us
  local copies, waits for them, and re-layouts: 1.67 us -> 0.71 us
    pallas_call x1, Pallas kernels: 60 us -> 58.4 us  [body(): pl.pallas_call(functools.partial(kernel, n_amp, n_int), out_shape=jax.Sha...]
    unnamed x1, local copies, waits for them, and re-layouts: 1.67 us -> 0.71 us
where the time goes in v4:
time: 59.2 us; the launch traced here: 59.1 us
  Pallas kernels  58.4 us (99%)
  local copies, waits for them, and re-layouts  0.71 us (1%)
    pallas_call x1, Pallas kernels, body(): pl.pallas_call(functools.partial(kernel, n_amp, n_int), out_shape=jax.Sha...  58.4 us

profile of v4, /device:TPU:1, one launch (start us, length us, event | category | flops | bytes accessed | tf_op | source)
XLA Modules:
  0.0 59.1 jit_solution(5309512887200057029)
XLA Ops:
  0.0 58.4 %shard_map.55 = bf16[8,128,128]{2,1,0:T(8,128)(2,1)S(1)} custom-call(bf16[8,128,128]{2,1,0:T(8,128)(2,1)} %amps.1, bf16[8,2,128,128]{3,2,1,0:T(8,128)(2,1)} %integrals.1, bf16[1024,1024]{1,0:T(8,128)(2,1)} %hole_int.1, s32[1,64]{1,0:T(1,128)} %bitcast.1, s32[8,16]{1,0:T(8,128)} %slot_list.1), custom_call_target="tpu_custom_call" | custom-call | tf_op jit(solution)/shard_map/pallas_call | solution.py:319
  58.4 0.7 %copy.7 = bf16[8,128,128]{2,1,0:T(8,128)(2,1)} copy(bf16[8,128,128]{2,1,0:T(8,128)(2,1)S(1)} %shard_map.55) | data formatting | bytes 524288

commit v5 on v4

--- a/solution.py
+++ b/solution.py
@@ -10,6 +10,7 @@
 MESH = pl.DeviceIdType.MESH
 NZ = 16
 REACH = 5
+FIRST = 2
 CT = 2
 STAGE = ((0, 1, 0, 1), (1, 0, 1, 0), (3,) * 4, (2,) * 4, (2,) * 4, (3,) * 4, (3,) * 4, (3,) * 4)
 
@@ -139,6 +140,13 @@
                 if reach + h < half or j // (ny // 2) == d:
                     beyond[h, j, d] = len(named)
                     named.append((d, reach, j, h - 2 * d * h))
+    n_even = len(named)
+    top = half - reach
+    uneven = []
+    for j in range(ny // 2):
+        uneven.append(len(named))
+        named.append((1, reach, j, -top))
+    target_first = [(z + shift + nz) % nz < FIRST for shift in (top, -top)]
 
     def z_of(d, t, shift):
         return (z + shift + (t if d else -t) + nz) % nz
@@ -243,11 +251,23 @@
     for d in range(2):
         to_smem(d, reach).wait()
     by_y = (2, 1, 3, 0)
-    for h in range(half - reach, 0, -1):
+
+    def far_send(d, h):
+        for j in by_y:
+            if (h, j, d) in beyond:
+                n_send(beyond[h, j, d])
+
+    def far_uneven():
+        for n in uneven:
+            n_send(n)
+
+    pl.when(jnp.logical_not(target_first[0]))(functools.partial(far_send, 0, top))
+    far_send(1, top)
+    pl.when(target_first[1])(far_uneven)
+    for h in range(top - 1, 0, -1):
         for j in by_y:
             for d in range(2):
-                if (h, j, d) in beyond:
-                    n_send(beyond[h, j, d])
+                n_send(beyond[h, j, d])
     for j in by_y[:-1]:
         for d in range(2):
             n_send(near[d, reach][j - 1])
@@ -258,7 +278,7 @@
 
     own[0].wait()
     own[4].wait()
-    arrival(picked, yr)
+    arrival(picked.at[pl.ds(0, n_even)], yr)
 
     knz = slot_of.shape[1]
     per = knz // n_int
@@ -275,7 +295,14 @@
         for t in range(1, reach + 1):
             arrival(bufs[d][t], zs)
     arrival(meta.at[:, pl.ds(1, reach)], ms)
-    arrival(picked, ys)
+    n_split = ny // 2
+
+    def sent_split():
+        arrival(picked.at[pl.ds(0, n_split)], ys)
+
+    arrival(picked.at[pl.ds(0, n_even - n_split)], ys)
+    pl.when(jnp.logical_not(target_first[0]))(sent_split)
+    pl.when(target_first[1])(sent_split)
     for sem, ref in ((0, all_amps), (1, all_int)):
         arrival(ref.at[pl.ds(0, n_int - 1)], xs.at[sem])
 
@@ -292,7 +319,7 @@
     hbm = pl.BlockSpec(memory_space=pltpu.HBM)
     operands = (amps, integrals, hole_int, row_list, slot_of)
     reach = REACH
-    n_named = (2 * reach + 1) * (ny - 1) + (2 * (half - reach) - 1) * ny
+    n_named = (2 * reach + 1) * (ny - 1) + (2 * (half - reach) - 1) * ny + ny // 2
     scratch = [tiles] * (2 * reach)
     scratch += [
         tiles,

time: 59.2 us -> 58.2 us (0.983)
  the two profiles are of different devices: /device:TPU:1 before, /device:TPU:4 now
where the time goes in v5:
time: 58.2 us; the launch traced here: 58 us
  Pallas kernels  57.3 us (98%)
  local copies, waits for them, and re-layouts  0.71 us (1%)
    pallas_call x1, Pallas kernels, body(): pl.pallas_call(functools.partial(kernel, n_amp, n_int), out_shape=jax.Sha...  57.3 us

profile of v5, /device:TPU:4, one launch (start us, length us, event | category | flops | bytes accessed | tf_op | source)
XLA Modules:
  0.0 58.0 jit_solution(7523950586041999155)
XLA Ops:
  0.0 57.3 %shard_map.55 = bf16[8,128,128]{2,1,0:T(8,128)(2,1)S(1)} custom-call(bf16[8,128,128]{2,1,0:T(8,128)(2,1)} %amps.1, bf16[8,2,128,128]{3,2,1,0:T(8,128)(2,1)} %integrals.1, bf16[1024,1024]{1,0:T(8,128)(2,1)} %hole_int.1, s32[1,64]{1,0:T(1,128)} %bitcast.1, s32[8,16]{1,0:T(8,128)} %slot_list.1), custom_call_target="tpu_custom_call" | custom-call | tf_op jit(solution)/shard_map/pallas_call | solution.py:346
  57.3 0.7 %copy.7 = bf16[8,128,128]{2,1,0:T(8,128)(2,1)} copy(bf16[8,128,128]{2,1,0:T(8,128)(2,1)S(1)} %shard_map.55) | data formatting | bytes 524288

commit v6 on v5

--- a/solution.py
+++ b/solution.py
@@ -246,8 +246,8 @@
                     to_smem(d, t).start()
             if t > 1:
                 name_part(t - 1, c)
-        if t >= reach - 3 and t < reach:
-            x_stage(t - reach + 3)
+        if t == reach - 1:
+            x_stage(0)
     for d in range(2):
         to_smem(d, reach).wait()
     by_y = (2, 1, 3, 0)
@@ -273,6 +273,8 @@
             n_send(near[d, reach][j - 1])
     for d in range(2):
         keep_own(d, reach)
+    x_stage(1)
+    x_stage(2)
     x_stage(3)
     hole_part()
 

time: 58.2 us -> 58.2 us (level)
  no operation moved by 1% of the time
where the time goes in v6:
time: 58.2 us; the launch traced here: 58 us
  Pallas kernels  57.3 us (98%)
  local copies, waits for them, and re-layouts  0.71 us (1%)
    pallas_call x1, Pallas kernels, body(): pl.pallas_call(functools.partial(kernel, n_amp, n_int), out_shape=jax.Sha...  57.3 us

profile of v6, /device:TPU:4, one launch (start us, length us, event | category | flops | bytes accessed | tf_op | source)
XLA Modules:
  0.0 58.0 jit_solution(13564442969573887641)
XLA Ops:
  0.0 57.3 %shard_map.55 = bf16[8,128,128]{2,1,0:T(8,128)(2,1)S(1)} custom-call(bf16[8,128,128]{2,1,0:T(8,128)(2,1)} %amps.1, bf16[8,2,128,128]{3,2,1,0:T(8,128)(2,1)} %integrals.1, bf16[1024,1024]{1,0:T(8,128)(2,1)} %hole_int.1, s32[1,64]{1,0:T(1,128)} %bitcast.1, s32[8,16]{1,0:T(8,128)} %slot_list.1), custom_call_target="tpu_custom_call" | custom-call | tf_op jit(solution)/shard_map/pallas_call | solution.py:348
  57.3 0.7 %copy.7 = bf16[8,128,128]{2,1,0:T(8,128)(2,1)} copy(bf16[8,128,128]{2,1,0:T(8,128)(2,1)S(1)} %shard_map.55) | data formatting | bytes 524288
